TPU v7x, 32 devices: a whole 2x2x4 slice. The times are simulated.
32 devices in a mesh: grp: 2 (over x), feat: 8 (over z, y), tok: 2 (over core).
Axes of the slice: x: 2, y: 2, z: 4, core: 2. Of those that a mesh axis runs over, the one named last changes fastest.
Arguments:
- states: bfloat16 [4096, 8192], P(('grp', 'tok'), 'feat'), parts along dimension 0, may hold values from -6 to 6
Outputs:
- covariance: float32 [16384, 8192], P(('grp', 'tok'), 'feat'), parts along dimension 0
There are 2 independent parts, one for each index of `grp`. A program takes and returns all parts, laid end to end along the dimension named above; each array names one. Nothing has to cross between parts.
All inputs are finite; a program needn't handle non-finite values.
Results may differ from a plain program's by a relative error of at most 0.0003.
Values may be sent and summed in bfloat16 or wider, within the bound.
A program may use at most 192 MiB of HBM per device.

v0:
```python
import jax
import jax.numpy as jnp
from jax import lax
from jax.sharding import PartitionSpec as P


def contract(left, right):
    return lax.dot_general(
        left, right, (((0,), (0,)), ((), ())), preferred_element_type=jnp.float32
    )


def shards(states):
    token_count = states.shape[0] * lax.axis_size("tok")
    partial_rows = contract(lax.all_gather(states, "feat", axis=1, tiled=True), states)
    summed = lax.psum_scatter(partial_rows, "tok", scatter_dimension=0, tiled=True)
    return summed / jnp.float32(token_count)


def solution(mesh):
    placed = (P(("grp", "tok"), "feat"),)
    return jax.shard_map(
        shards, mesh=mesh, in_specs=placed, out_specs=P(("grp", "tok"), "feat"), check_vma=False
    )
```

profile of v0, /device:TPU:0, one launch (start us, length us, event | category | flops | bytes accessed | tf_op | source)
XLA Modules:
  0.0 330.3 jit_solution(3277223404090792383)
XLA Ops:
  6.5 0.0 all-gather.2.cloned.1.call-start
  6.5 0.7 all-gather.2.cloned.1.call-update
  7.3 0.0 reduce-scatter.2.cloned.1.call-start
  7.3 232.6 %all-gather.2.cloned.1.call-done = bf16[1024,8192]{1,0:T(8,128)(2,1)} async-done(((bf16[1024,1024]{1,0:T(8,128)(2,1)}), bf16[1024,8192]{1,0:T(8,128)(2,1)}) %all-gather.2.cloned.1.call-update) | async-done | bytes 16777232 | tf_op jit(solution)/shard_map/all_gather | solution.py:15
  239.9 27.7 %fusion = f32[8192,1024]{1,0:T(8,128)} fusion(bf16[1024,8192]{1,0:T(8,128)(2,1)} %all-gather.2.cloned.1.call-done, bf16[1024,1024]{1,0:T(8,128)(2,1)} %param.1), kind=kOutput, calls=%fused_computation.1 | convolution fusion | flops 17179869184 | bytes 52428800 | tf_op jit(solution)/shard_map/dot_general | solution.py:8
  267.6 0.0 reduce-scatter.2.cloned.1.call-update
  267.6 43.4 %reduce-scatter.2.cloned.1.call-done = f32[4096,1024]{1,0:T(8,128)} async-done(((f32[8192,1024]{1,0:T(8,128)}), f32[4096,1024]{1,0:T(8,128)}) %reduce-scatter.2.cloned.1.call-update) | async-done | bytes 16777232 | tf_op jit(solution)/shard_map/reduce_scatter | solution.py:16
  311.1 12.4 %broadcast_multiply_fusion = f32[4096,1024]{1,0:T(8,128)} fusion(f32[4096,1024]{1,0:T(8,128)} %reduce-scatter.2.cloned.1.call-done), kind=kLoop, calls=%fused_computation | loop fusion | flops 4194304 | bytes 33554432 | tf_op jit(solution)/shard_map/div | solution.py:17
Async XLA Ops:
  6.5 233.3 %all-gather.2.cloned.1.call-start = ((), (), s32[]{:S(2)}) async-start(), calls=%async_computation.1 | async-start | bytes 18874368 | tf_op jit(solution)/shard_map/all_gather | solution.py:15
  7.3 303.8 %reduce-scatter.2.cloned.1.call-start = ((), (), s32[]{:S(2)}) async-start(), calls=%async_computation.2 | async-start | bytes 50331648 | tf_op jit(solution)/shard_map/reduce_scatter | solution.py:16
Sparse Core Ops, SparseCore 0:
  9.5 230.2 all-gather.1
  267.7 43.2 reduce-scatter.1
where the time goes:
time: 330 us
  waiting for transfers between devices  277 us (84%)
  matrix products  27.7 us (8%)
  between operations  13.4 us (4%)
  other arithmetic  12.4 us (4%)
    all_gather x1, waiting for transfers between devices, shards(): lax.all_gather(states, 'feat', axis=1, tiled=True)  233 us
    reduce_scatter x1, waiting for transfers between devices, shards(): lax.psum_scatter(partial_rows, 'tok', scatter_dimension=0, tiled=True)  43.4 us
    dot_general x1, matrix products, contract(): lax.dot_general(left, right, (((0,), (0,)), ((), ())), preferred_element_...  27.7 us
    div x1, other arithmetic, shards(): return summed / jnp.float32(token_count)  12.4 us
  transfers between devices with their start and end apart: 2, of which 2 were waited for; matrix products, arithmetic and copies ran while one was open for 0% of the time, Pallas kernels for 0%

commit v1 on v0

v1 whole, which is shorter than its diff:
```python
import functools

import jax
import jax.numpy as jnp
from jax import lax
from jax.experimental import pallas as pl
from jax.experimental.pallas import tpu as pltpu
from jax.sharding import PartitionSpec as P

MESH = pl.DeviceIdType.MESH


def feature_of(place, n, snake):
    if not snake:
        return place
    back = place // (n // 2)
    return (1 - back) * 2 * place + back * (2 * (n - 1 - place) + 1)


def place_of(feature, n, snake):
    if not snake:
        return feature
    odd = feature % 2
    return (1 - odd) * (feature // 2) + odd * (n - 1 - feature // 2)


def kernel(
    n, pieces, snake, tokens, x_ref, out_ref, held, other, stage,
    ring_send, ring_recv, pair_send, pair_recv, load_sem, store_sem,
):
    width = held.shape[-1]
    block = width * pieces
    half = n // 2
    me = lax.axis_index("feat")
    tok = lax.axis_index("tok")
    place = place_of(me, n, snake)

    def at_distance(steps):
        return feature_of((place + steps + n) % n, n, snake)

    def origin(arrival, piece):
        return at_distance((2 * (piece % 2) - 1) * arrival)

    def partner(piece):
        return at_distance(1 - 2 * (piece % 2))

    def ring(arrival, piece, feature, src=None):
        return pltpu.make_async_remote_copy(
            src_ref=held.at[feature, piece] if src is None else src,
            dst_ref=held.at[feature, piece],
            send_sem=ring_send.at[arrival - 1, piece],
            recv_sem=ring_recv.at[arrival - 1, piece],
            device_id={"feat": partner(piece)},
            device_id_type=MESH,
        )

    def pair(slot, piece, src):
        return pltpu.make_async_remote_copy(
            src_ref=src,
            dst_ref=other.at[slot, piece],
            send_sem=pair_send.at[slot, piece],
            recv_sem=pair_recv.at[slot, piece],
            device_id={"tok": 1 - tok},
            device_id_type=MESH,
        )

    def load(piece):
        return pltpu.make_async_copy(
            x_ref.at[:, pl.ds(piece * width, width)], held.at[me, piece], load_sem.at[piece]
        )

    def store(slot, piece):
        rows = pl.ds(pl.multiple_of(slot * block + piece * width, width), width)
        return pltpu.make_async_copy(
            stage.at[slot, piece], out_ref.at[rows, :], store_sem.at[slot, piece]
        )

    barrier = pltpu.get_barrier_semaphore()
    for where in ({"feat": at_distance(1)}, {"feat": at_distance(-1)}, {"tok": 1 - tok}):
        pl.semaphore_signal(barrier, inc=1, device_id=where, device_id_type=MESH)
    pl.semaphore_wait(barrier, 3)

    for piece in range(pieces):
        part = x_ref.at[:, pl.ds(piece * width, width)]
        ring(1, piece, me, part).start()
        load(piece).start()
    for piece in range(pieces):
        pair(half, piece, x_ref.at[:, pl.ds(piece * width, width)]).start()
    for piece in range(pieces):
        load(piece).wait()
    for piece in range(pieces):
        pair(half, piece, held.at[me, piece]).wait_recv()

    def multiply(feature, piece, from_other):
        slot = feature % half
        first = held[feature, piece].T
        second = other[from_other, piece].T
        for column in range(pieces):
            total = jnp.dot(first, held[me, column], preferred_element_type=jnp.float32)
            total += jnp.dot(second, other[half, column], preferred_element_type=jnp.float32)
            stage[slot, piece, :, column * width:(column + 1) * width] = total / jnp.float32(tokens)
        store(slot, piece).start()

    def compute(arrival, piece):
        feature = origin(arrival, piece)
        slot = feature % half

        @pl.when(feature // half == tok)
        def _():
            @pl.when(arrival > 0)
            def _():
                pair(slot, piece, held.at[feature, piece]).wait_recv()

            own = 1 - (arrival + n - 1) // n
            multiply(feature, piece, own * half + (1 - own) * slot)

    @pl.loop(1, n)
    def _(arrival):
        @pl.loop(0, pieces)
        def _(piece):
            feature = origin(arrival, piece)
            ring(arrival, piece, feature).wait_recv()

            @pl.when(arrival < n - 1)
            def _():
                ring(arrival + 1, piece, feature).start()

            @pl.when(feature // half != tok)
            def _():
                pair(feature % half, piece, held.at[feature, piece]).start()

            compute(arrival - 1, piece)

    @pl.loop(0, pieces)
    def _(piece):
        compute(n - 1, piece)

    @pl.loop(0, pieces)
    def _(piece):
        @pl.loop(1, n)
        def _(arrival):
            feature = origin(arrival, piece)
            ring(arrival, piece, feature).wait_send()

            @pl.when(feature // half != tok)
            def _():
                pair(feature % half, piece, held.at[feature, piece]).wait_send()

        pair(half, piece, held.at[me, piece]).wait_send()

        @pl.loop(0, half)
        def _(slot):
            store(slot, piece).wait()


def solution(mesh):
    n = mesh.shape["feat"]
    snake = mesh.shape["grp"] == 2

    def shards(states):
        rows, block = states.shape
        tokens = rows * mesh.shape["tok"]
        pieces = max(2, min(4, block // 128))
        width = block // pieces
        half = n // 2
        return pl.pallas_call(
            functools.partial(kernel, n, pieces, snake, tokens),
            out_shape=jax.ShapeDtypeStruct((half * block, block), jnp.float32),
            in_specs=[pl.BlockSpec(memory_space=pl.ANY)],
            out_specs=pl.BlockSpec(memory_space=pl.ANY),
            scratch_shapes=[
                pltpu.VMEM((n, pieces, rows, width), states.dtype),
                pltpu.VMEM((half + 1, pieces, rows, width), states.dtype),
                pltpu.VMEM((half, pieces, width, block), jnp.float32),
                pltpu.SemaphoreType.DMA((n - 1, pieces)),
                pltpu.SemaphoreType.DMA((n - 1, pieces)),
                pltpu.SemaphoreType.DMA((half + 1, pieces)),
                pltpu.SemaphoreType.DMA((half + 1, pieces)),
                pltpu.SemaphoreType.DMA((pieces,)),
                pltpu.SemaphoreType.DMA((half, pieces)),
            ],
            compiler_params=pltpu.CompilerParams(
                collective_id=0, has_side_effects=True, vmem_limit_bytes=56 * 2**20
            ),
            cost_estimate=pl.CostEstimate(
                flops=2 * half * block * block * tokens,
                bytes_accessed=half * block * block * 4 + rows * block * 2,
                transcendentals=0,
            ),
        )(states)

    placed = P(("grp", "tok"), "feat")
    return jax.shard_map(
        shards, mesh=mesh, in_specs=(placed,), out_specs=placed, check_vma=False
    )
```

time: 330 us -> 183 us (0.55)
  waiting for transfers between devices: 277 us -> 0 us
  Pallas kernels: 0 us -> 171 us
  matrix products: 27.7 us -> 0 us
  between operations: 13.4 us -> 0.01 us
  other arithmetic: 12.4 us -> 0 us
  local copies, waits for them, and re-layouts: 0 us -> 12 us
    all_gather x1 -> x0, waiting for transfers between devices: 233 us -> none  [shards(): lax.all_gather(states, 'feat', axis=1, tiled=True)]
    pallas_call x0 -> x1, Pallas kernels: none -> 171 us  [shards(): pl.pallas_call(functools.partial(kernel, n, pieces, snake, tokens), out_s...]
    reduce_scatter x1 -> x0, waiting for transfers between devices: 43.4 us -> none  [shards(): lax.psum_scatter(partial_rows, 'tok', scatter_dimension=0, tiled=True)]
    dot_general x1 -> x0, matrix products: 27.7 us -> none  [contract(): lax.dot_general(left, right, (((0,), (0,)), ((), ())), preferred_element_...]
    div x1 -> x0, other arithmetic: 12.4 us -> none  [shards(): return summed / jnp.float32(token_count)]
    unnamed x0 -> x1, local copies, waits for them, and re-layouts: none -> 12 us
  transfers between devices with their start and end apart: 2 -> 0, of which waited for: 2 -> 0; matrix products, arithmetic and copies ran while one was open for 0% -> 0% of each run, Pallas kernels for 0% -> 0%
where the time goes in v1:
time: 183 us
  Pallas kernels  171 us (93%)
  local copies, waits for them, and re-layouts  12 us (7%)
    pallas_call x1, Pallas kernels, shards(): pl.pallas_call(functools.partial(kernel, n, pieces, snake, tokens), out_s...  171 us
    unnamed x1, local copies, waits for them, and re-layouts  12 us

profile of v1, /device:TPU:0, one launch (start us, length us, event | category | flops | bytes accessed | tf_op | source)
XLA Modules:
  0.0 183.1 jit_solution(2456890384547908105)
XLA Ops:
  0.0 171.1 %shard_map.17 = f32[4096,1024]{1,0:T(8,128)} custom-call(bf16[1024,1024]{1,0:T(8,128)(2,1)} %x_ref.1), custom_call_target="tpu_custom_call" | custom-call | flops 17179869184 | bytes 18874368 | tf_op jit(solution)/shard_map/pallas_call | solution.py:166
  171.1 12.0 %copy.3 = f32[4096,1024]{1,0:T(8,128)} copy(f32[4096,1024]{1,0:T(8,128)} %shard_map.17) | data formatting | bytes 33554432

commit v2 on v1

--- a/solution.py
+++ b/solution.py
@@ -25,8 +25,8 @@
 
 
 def kernel(
-    n, pieces, snake, tokens, x_ref, out_ref, held, other, stage,
-    ring_send, ring_recv, pair_send, pair_recv, load_sem, store_sem,
+    n, pieces, snake, tokens, x_ref, stage, held, other,
+    ring_send, ring_recv, pair_send, pair_recv, load_sem,
 ):
     width = held.shape[-1]
     block = width * pieces
@@ -69,12 +69,6 @@
             x_ref.at[:, pl.ds(piece * width, width)], held.at[me, piece], load_sem.at[piece]
         )
 
-    def store(slot, piece):
-        rows = pl.ds(pl.multiple_of(slot * block + piece * width, width), width)
-        return pltpu.make_async_copy(
-            stage.at[slot, piece], out_ref.at[rows, :], store_sem.at[slot, piece]
-        )
-
     barrier = pltpu.get_barrier_semaphore()
     for where in ({"feat": at_distance(1)}, {"feat": at_distance(-1)}, {"tok": 1 - tok}):
         pl.semaphore_signal(barrier, inc=1, device_id=where, device_id_type=MESH)
@@ -99,7 +93,6 @@
             total = jnp.dot(first, held[me, column], preferred_element_type=jnp.float32)
             total += jnp.dot(second, other[half, column], preferred_element_type=jnp.float32)
             stage[slot, piece, :, column * width:(column + 1) * width] = total / jnp.float32(tokens)
-        store(slot, piece).start()
 
     def compute(arrival, piece):
         feature = origin(arrival, piece)
@@ -148,9 +141,22 @@
 
         pair(half, piece, held.at[me, piece]).wait_send()
 
-        @pl.loop(0, half)
-        def _(slot):
-            store(slot, piece).wait()
+
+def write_out(pieces, product_ref, out_ref, sem):
+    half, _, width, _ = product_ref.shape
+    copies = [
+        pltpu.make_async_copy(
+            product_ref.at[slot, piece],
+            out_ref.at[pl.ds((slot * pieces + piece) * width, width), :],
+            sem.at[slot, piece],
+        )
+        for slot in range(half)
+        for piece in range(pieces)
+    ]
+    for copy in copies:
+        copy.start()
+    for copy in copies:
+        copy.wait()
 
 
 def solution(mesh):
@@ -163,24 +169,22 @@
         pieces = max(2, min(4, block // 128))
         width = block // pieces
         half = n // 2
-        return pl.pallas_call(
+        product = pl.pallas_call(
             functools.partial(kernel, n, pieces, snake, tokens),
-            out_shape=jax.ShapeDtypeStruct((half * block, block), jnp.float32),
+            out_shape=pltpu.VMEM((half, pieces, width, block), jnp.float32),
             in_specs=[pl.BlockSpec(memory_space=pl.ANY)],
-            out_specs=pl.BlockSpec(memory_space=pl.ANY),
+            out_specs=pl.BlockSpec(memory_space=pltpu.VMEM),
             scratch_shapes=[
                 pltpu.VMEM((n, pieces, rows, width), states.dtype),
                 pltpu.VMEM((half + 1, pieces, rows, width), states.dtype),
-                pltpu.VMEM((half, pieces, width, block), jnp.float32),
                 pltpu.SemaphoreType.DMA((n - 1, pieces)),
                 pltpu.SemaphoreType.DMA((n - 1, pieces)),
                 pltpu.SemaphoreType.DMA((half + 1, pieces)),
                 pltpu.SemaphoreType.DMA((half + 1, pieces)),
                 pltpu.SemaphoreType.DMA((pieces,)),
-                pltpu.SemaphoreType.DMA((half, pieces)),
             ],
             compiler_params=pltpu.CompilerParams(
-                collective_id=0, has_side_effects=True, vmem_limit_bytes=56 * 2**20
+                collective_id=0, has_side_effects=True, vmem_limit_bytes=36 * 2**20
             ),
             cost_estimate=pl.CostEstimate(
                 flops=2 * half * block * block * tokens,
@@ -188,6 +192,14 @@
                 transcendentals=0,
             ),
         )(states)
+        return pl.pallas_call(
+            functools.partial(write_out, pieces),
+            out_shape=jax.ShapeDtypeStruct((half * block, block), jnp.float32),
+            in_specs=[pl.BlockSpec(memory_space=pltpu.VMEM)],
+            out_specs=pl.BlockSpec(memory_space=pl.ANY),
+            scratch_shapes=[pltpu.SemaphoreType.DMA((half, pieces))],
+            compiler_params=pltpu.CompilerParams(vmem_limit_bytes=2**20),
+        )(pltpu.with_memory_space_constraint(product, pltpu.VMEM))
 
     placed = P(("grp", "tok"), "feat")
     return jax.shard_map(

time: 183 us -> 177 us (0.967)
  local copies, waits for them, and re-layouts: 12 us -> 0 us
  Pallas kernels: 171 us -> 177 us
    unnamed x1 -> x0, local copies, waits for them, and re-layouts: 12 us -> none
    pallas_call x0 -> x1, Pallas kernels: none -> 5.96 us  [shards(): pl.pallas_call(functools.partial(write_out, pieces), out_shape=jax.ShapeD...]
where the time goes in v2:
time: 177 us
  Pallas kernels  177 us (100%)
    pallas_call x1, Pallas kernels, shards(): pl.pallas_call(functools.partial(kernel, n, pieces, snake, tokens), out_s...  171 us
    pallas_call x1, Pallas kernels, shards(): pl.pallas_call(functools.partial(write_out, pieces), out_shape=jax.ShapeD...  5.96 us

profile of v2, /device:TPU:0, one launch (start us, length us, event | category | flops | bytes accessed | tf_op | source)
XLA Modules:
  0.0 176.9 jit_solution(14990272272038894736)
XLA Ops:
  0.0 170.9 %shard_map.17.product_ref = f32[4,4,256,1024]{3,2,1,0:T(8,128)S(1)} custom-call(bf16[1024,1024]{1,0:T(8,128)(2,1)} %x_ref.1), custom_call_target="tpu_custom_call" | custom-call | flops 17179869184 | bytes 18874368 | tf_op jit(solution)/shard_map/pallas_call | solution.py:172
  170.9 6.0 %shard_map.18 = f32[4096,1024]{1,0:T(8,128)} custom-call(f32[4,4,256,1024]{3,2,1,0:T(8,128)S(1)} %shard_map.17.product_ref), custom_call_target="tpu_custom_call" | custom-call | tf_op jit(solution)/shard_map/pallas_call | solution.py:195

commit v3 on v1

v3 whole, which is shorter than its diff:
```python
import functools

import jax
import jax.numpy as jnp
from jax import lax
from jax.experimental import pallas as pl
from jax.experimental.pallas import tpu as pltpu
from jax.sharding import PartitionSpec as P

MESH = pl.DeviceIdType.MESH


def feature_of(place, n, snake):
    if not snake:
        return place
    back = place // (n // 2)
    return (1 - back) * 2 * place + back * (2 * (n - 1 - place) + 1)


def place_of(feature, n, snake):
    if not snake:
        return feature
    odd = feature % 2
    return (1 - odd) * (feature // 2) + odd * (n - 1 - feature // 2)


def position(n, snake):
    tok = lax.axis_index("tok")
    place = place_of(lax.axis_index("feat"), n, snake)

    def at_distance(steps):
        return feature_of((place + steps + n) % n, n, snake)

    def origin(arrival, piece):
        return at_distance((2 * (piece % 2) - 1) * arrival)

    return tok, at_distance, origin


def multiply(held, other, feature, piece, from_other, tokens, target):
    pieces, _, width = held.shape[1:]
    own = other.shape[0] - 1
    me = lax.axis_index("feat")
    first = held[feature, piece].T
    second = other[from_other, piece].T
    for column in range(pieces):
        total = jnp.dot(first, held[me, column], preferred_element_type=jnp.float32)
        total += jnp.dot(second, other[own, column], preferred_element_type=jnp.float32)
        target[:, column * width:(column + 1) * width] = total / jnp.float32(tokens)


def gather_and_multiply(
    n, snake, tokens, x_ref, product, held, other,
    ring_send, ring_recv, pair_send, pair_recv, load_sem,
):
    _, pieces, _, width = held.shape
    half = n // 2
    last = n - 1
    me = lax.axis_index("feat")
    tok, at_distance, origin = position(n, snake)

    def partner(piece):
        return at_distance(1 - 2 * (piece % 2))

    def ring(arrival, piece, feature, src=None):
        return pltpu.make_async_remote_copy(
            src_ref=held.at[feature, piece] if src is None else src,
            dst_ref=held.at[feature, piece],
            send_sem=ring_send.at[arrival - 1, piece],
            recv_sem=ring_recv.at[arrival - 1, piece],
            device_id={"feat": partner(piece)},
            device_id_type=MESH,
        )

    def across(piece, feature):
        return pltpu.make_async_remote_copy(
            src_ref=held.at[feature, piece],
            dst_ref=other.at[feature % half, piece],
            send_sem=ring_send.at[last - 1, piece],
            recv_sem=pair_recv.at[feature % half, piece],
            device_id={"feat": partner(piece), "tok": 1 - tok},
            device_id_type=MESH,
        )

    def pair(slot, piece, src):
        return pltpu.make_async_remote_copy(
            src_ref=src,
            dst_ref=other.at[slot, piece],
            send_sem=pair_send.at[slot, piece],
            recv_sem=pair_recv.at[slot, piece],
            device_id={"tok": 1 - tok},
            device_id_type=MESH,
        )

    def load(piece):
        return pltpu.make_async_copy(
            x_ref.at[:, pl.ds(piece * width, width)], held.at[me, piece], load_sem.at[piece]
        )

    barrier = pltpu.get_barrier_semaphore()
    for where in (
        {"feat": at_distance(1)},
        {"feat": at_distance(-1)},
        {"tok": 1 - tok},
        {"feat": at_distance(1), "tok": 1 - tok},
        {"feat": at_distance(-1), "tok": 1 - tok},
    ):
        pl.semaphore_signal(barrier, inc=1, device_id=where, device_id_type=MESH)
    pl.semaphore_wait(barrier, 5)

    for piece in range(pieces):
        part = x_ref.at[:, pl.ds(piece * width, width)]
        ring(1, piece, me, part).start()
        load(piece).start()
    for piece in range(pieces):
        pair(half, piece, x_ref.at[:, pl.ds(piece * width, width)]).start()
    for piece in range(pieces):
        load(piece).wait()
    for piece in range(pieces):
        pair(half, piece, held.at[me, piece]).wait_recv()

    def compute(arrival, piece):
        feature = origin(arrival, piece)
        slot = feature % half

        @pl.when(feature // half == tok)
        def _():
            @pl.when(arrival > 0)
            def _():
                pair(slot, piece, held.at[feature, piece]).wait_recv()

            own = 1 - (arrival + n - 1) // n
            from_other = own * half + (1 - own) * slot
            multiply(held, other, feature, piece, from_other, tokens, product.at[slot, piece])

    @pl.loop(1, last)
    def _(arrival):
        @pl.loop(0, pieces)
        def _(piece):
            feature = origin(arrival, piece)
            mine = feature // half == tok
            ring(arrival, piece, feature).wait_recv()

            @pl.when((arrival < last - 1) | mine)
            def _():
                ring(arrival + 1, piece, feature).start()

            @pl.when((arrival == last - 1) & (feature // half != tok))
            def _():
                across(piece, feature).start()

            @pl.when(feature // half != tok)
            def _():
                pair(feature % half, piece, held.at[feature, piece]).start()

            compute(arrival - 1, piece)

    @pl.loop(0, pieces)
    def _(piece):
        compute(last - 1, piece)

    @pl.loop(0, pieces)
    def _(piece):
        @pl.loop(1, last)
        def _(arrival):
            feature = origin(arrival, piece)
            ring(arrival, piece, feature).wait_send()

            @pl.when(feature // half != tok)
            def _():
                pair(feature % half, piece, held.at[feature, piece]).wait_send()

        pair(half, piece, held.at[me, piece]).wait_send()

    @pl.loop(0, pieces)
    def _(piece):
        feature = origin(last, piece)
        ring(last, piece, feature).wait_send()

        @pl.when(feature // half == tok)
        def _():
            ring(last, piece, feature).wait_recv()
            pair(feature % half, piece, held.at[feature, piece]).wait_recv()


def finish(n, snake, tokens, product, held, other, out_ref, late, sem):
    half, pieces, width, _ = product.shape
    tok, _, origin = position(n, snake)

    def store(slot, piece, src):
        rows = pl.ds(pl.multiple_of((slot * pieces + piece) * width, width), width)
        return pltpu.make_async_copy(src, out_ref.at[rows, :], sem.at[slot, piece])

    @pl.loop(0, half)
    def _(slot):
        @pl.loop(0, pieces)
        def _(piece):
            @pl.when(origin(n - 1, piece) != tok * half + slot)
            def _():
                store(slot, piece, product.at[slot, piece]).start()

    @pl.loop(0, pieces)
    def _(piece):
        feature = origin(n - 1, piece)
        slot = feature % half

        @pl.when(feature // half == tok)
        def _():
            multiply(held, other, feature, piece, slot, tokens, late.at[piece])
            store(slot, piece, late.at[piece]).start()

    @pl.loop(0, half)
    def _(slot):
        @pl.loop(0, pieces)
        def _(piece):
            store(slot, piece, product.at[slot, piece]).wait()


def solution(mesh):
    n = mesh.shape["feat"]
    snake = mesh.shape["grp"] == 2

    def shards(states):
        rows, block = states.shape
        tokens = rows * mesh.shape["tok"]
        pieces = max(2, min(4, block // 128))
        width = block // pieces
        half = n // 2
        gathered = pl.pallas_call(
            functools.partial(gather_and_multiply, n, snake, tokens),
            out_shape=(
                pltpu.VMEM((half, pieces, width, block), jnp.float32),
                pltpu.VMEM((n, pieces, rows, width), states.dtype),
                pltpu.VMEM((half + 1, pieces, rows, width), states.dtype),
            ),
            in_specs=[pl.BlockSpec(memory_space=pl.ANY)],
            out_specs=(pl.BlockSpec(memory_space=pltpu.VMEM),) * 3,
            scratch_shapes=[
                pltpu.SemaphoreType.DMA((n - 1, pieces)),
                pltpu.SemaphoreType.DMA((n - 1, pieces)),
                pltpu.SemaphoreType.DMA((half + 1, pieces)),
                pltpu.SemaphoreType.DMA((half + 1, pieces)),
                pltpu.SemaphoreType.DMA((pieces,)),
            ],
            compiler_params=pltpu.CompilerParams(
                collective_id=0, has_side_effects=True, vmem_limit_bytes=8 * 2**20
            ),
            cost_estimate=pl.CostEstimate(
                flops=2 * half * block * block * tokens,
                bytes_accessed=half * block * block * 4 + rows * block * 2,
                transcendentals=0,
            ),
        )(states)
        return pl.pallas_call(
            functools.partial(finish, n, snake, tokens),
            out_shape=jax.ShapeDtypeStruct((half * block, block), jnp.float32),
            in_specs=[pl.BlockSpec(memory_space=pltpu.VMEM)] * 3,
            out_specs=pl.BlockSpec(memory_space=pl.ANY),
            scratch_shapes=[
                pltpu.VMEM((pieces, width, block), jnp.float32),
                pltpu.SemaphoreType.DMA((half, pieces)),
            ],
            compiler_params=pltpu.CompilerParams(vmem_limit_bytes=10 * 2**20),
        )(*(pltpu.with_memory_space_constraint(part, pltpu.VMEM) for part in gathered))

    placed = P(("grp", "tok"), "feat")
    return jax.shard_map(
        shards, mesh=mesh, in_specs=(placed,), out_specs=placed, check_vma=False
    )
```

time: 183 us -> 172 us (0.940)
  local copies, waits for them, and re-layouts: 12 us -> 1.59 us
    unnamed x1 -> x2, local copies, waits for them, and re-layouts: 12 us -> 1.59 us
    pallas_call x1 -> x2, Pallas kernels: 171 us -> 171 us  [the longest x1 164 us: shards(): pl.pallas_call(functools.partial(gather_and_multiply, n, snake, tokens),...]
where the time goes in v3:
time: 172 us
  Pallas kernels  171 us (99%)
    pallas_call x1, Pallas kernels, shards(): pl.pallas_call(functools.partial(gather_and_multiply, n, snake, tokens),...  164 us
    pallas_call x1, Pallas kernels, shards(): pl.pallas_call(functools.partial(finish, n, snake, tokens), out_shape=jax...  6.74 us

profile of v3, /device:TPU:0, one launch (start us, length us, event | category | flops | bytes accessed | tf_op | source)
XLA Modules:
  0.0 172.2 jit_solution(17696560094419676011)
XLA Ops:
  0.0 0.0 copy-start
  0.0 1.6 copy-done
  1.6 163.9 %shard_map.17 = (f32[4,4,256,1024]{3,2,1,0:T(8,128)S(1)}, bf16[8,4,1024,256]{3,2,1,0:T(8,128)(2,1)S(1)}, bf16[5,4,1024,256]{3,2,1,0:T(8,128)(2,1)S(1)}) custom-call(bf16[1024,1024]{1,0:T(8,128)(2,1)S(1)} %copy-done), custom_call_target="tpu_custom_call" | custom-call | flops 17179869184 | bytes 18874368 | tf_op jit(solution)/shard_map/pallas_call | solution.py:229
  165.5 6.7 %shard_map.18 = f32[4096,1024]{1,0:T(8,128)} custom-call(f32[4,4,256,1024]{3,2,1,0:T(8,128)S(1)} %get-tuple-element.8.product, bf16[8,4,1024,256]{3,2,1,0:T(8,128)(2,1)S(1)} %get-tuple-element.9.held, bf16[5,4,1024,256]{3,2,1,0:T(8,128)(2,1)S(1)} %get-tuple-element.10.other), custom_call_target="tpu_custom_call" | custom-call | tf_op jit(solution)/shard_map/pallas_call | solution.py:254
Async XLA Ops:
  0.0 1.6 copy-start

commit v4 on v3

--- a/solution.py
+++ b/solution.py
@@ -243,7 +243,7 @@
                 pltpu.SemaphoreType.DMA((pieces,)),
             ],
             compiler_params=pltpu.CompilerParams(
-                collective_id=0, has_side_effects=True, vmem_limit_bytes=8 * 2**20
+                collective_id=0, has_side_effects=True, vmem_limit_bytes=10 * 2**20
             ),
             cost_estimate=pl.CostEstimate(
                 flops=2 * half * block * block * tokens,

time: 172 us -> 171 us (level)
  no operation moved by 1% of the time
where the time goes in v4:
time: 171 us
  Pallas kernels  171 us (100%)
    pallas_call x1, Pallas kernels, shards(): pl.pallas_call(functools.partial(gather_and_multiply, n, snake, tokens),...  164 us
    pallas_call x1, Pallas kernels, shards(): pl.pallas_call(functools.partial(finish, n, snake, tokens), out_shape=jax...  6.75 us

profile of v4, /device:TPU:0, one launch (start us, length us, event | category | flops | bytes accessed | tf_op | source)
XLA Modules:
  0.0 170.8 jit_solution(7552975090473244638)
XLA Ops:
  0.0 164.0 %shard_map.17 = (f32[4,4,256,1024]{3,2,1,0:T(8,128)S(1)}, bf16[8,4,1024,256]{3,2,1,0:T(8,128)(2,1)S(1)}, bf16[5,4,1024,256]{3,2,1,0:T(8,128)(2,1)S(1)}) custom-call(bf16[1024,1024]{1,0:T(8,128)(2,1)} %x_ref.1), custom_call_target="tpu_custom_call" | custom-call | flops 17179869184 | bytes 18874368 | tf_op jit(solution)/shard_map/pallas_call | solution.py:229
  164.0 6.8 %shard_map.18 = f32[4096,1024]{1,0:T(8,128)} custom-call(f32[4,4,256,1024]{3,2,1,0:T(8,128)S(1)} %get-tuple-element.8.product, bf16[8,4,1024,256]{3,2,1,0:T(8,128)(2,1)S(1)} %get-tuple-element.9.held, bf16[5,4,1024,256]{3,2,1,0:T(8,128)(2,1)S(1)} %get-tuple-element.10.other), custom_call_target="tpu_custom_call" | custom-call | tf_op jit(solution)/shard_map/pallas_call | solution.py:254

commit v5 on v4

--- a/solution.py
+++ b/solution.py
@@ -161,6 +161,20 @@
 
     @pl.loop(0, pieces)
     def _(piece):
+        feature = origin(last, piece)
+        slot = feature % half
+
+        @pl.when(feature // half == tok)
+        def _():
+            ring(last, piece, feature).wait_recv()
+            pair(slot, piece, held.at[feature, piece]).wait_recv()
+
+            @pl.when(piece < pieces // 2)
+            def _():
+                multiply(held, other, feature, piece, slot, tokens, product.at[slot, piece])
+
+    @pl.loop(0, pieces)
+    def _(piece):
         @pl.loop(1, last)
         def _(arrival):
             feature = origin(arrival, piece)
@@ -174,13 +188,7 @@
 
     @pl.loop(0, pieces)
     def _(piece):
-        feature = origin(last, piece)
-        ring(last, piece, feature).wait_send()
-
-        @pl.when(feature // half == tok)
-        def _():
-            ring(last, piece, feature).wait_recv()
-            pair(feature % half, piece, held.at[feature, piece]).wait_recv()
+        ring(last, piece, origin(last, piece)).wait_send()
 
 
 def finish(n, snake, tokens, product, held, other, out_ref, late, sem):
@@ -195,11 +203,11 @@
     def _(slot):
         @pl.loop(0, pieces)
         def _(piece):
-            @pl.when(origin(n - 1, piece) != tok * half + slot)
+            @pl.when((piece < pieces // 2) | (origin(n - 1, piece) != tok * half + slot))
             def _():
                 store(slot, piece, product.at[slot, piece]).start()
 
-    @pl.loop(0, pieces)
+    @pl.loop(pieces // 2, pieces)
     def _(piece):
         feature = origin(n - 1, piece)
         slot = feature % half

time: 171 us -> 171 us (level)
  no operation moved by 1% of the time
where the time goes in v5:
time: 171 us
  Pallas kernels  171 us (100%)
    pallas_call x1, Pallas kernels, shards(): pl.pallas_call(functools.partial(gather_and_multiply, n, snake, tokens),...  165 us
    pallas_call x1, Pallas kernels, shards(): pl.pallas_call(functools.partial(finish, n, snake, tokens), out_shape=jax...  6.01 us

profile of v5, /device:TPU:0, one launch (start us, length us, event | category | flops | bytes accessed | tf_op | source)
XLA Modules:
  0.0 170.7 jit_solution(7317702751548274426)
XLA Ops:
  0.0 164.7 %shard_map.17 = (f32[4,4,256,1024]{3,2,1,0:T(8,128)S(1)}, bf16[8,4,1024,256]{3,2,1,0:T(8,128)(2,1)S(1)}, bf16[5,4,1024,256]{3,2,1,0:T(8,128)(2,1)S(1)}) custom-call(bf16[1024,1024]{1,0:T(8,128)(2,1)} %x_ref.1), custom_call_target="tpu_custom_call" | custom-call | flops 17179869184 | bytes 18874368 | tf_op jit(solution)/shard_map/pallas_call | solution.py:237
  164.7 6.0 %shard_map.18 = f32[4096,1024]{1,0:T(8,128)} custom-call(f32[4,4,256,1024]{3,2,1,0:T(8,128)S(1)} %get-tuple-element.8.product, bf16[8,4,1024,256]{3,2,1,0:T(8,128)(2,1)S(1)} %get-tuple-element.9.held, bf16[5,4,1024,256]{3,2,1,0:T(8,128)(2,1)S(1)} %get-tuple-element.10.other), custom_call_target="tpu_custom_call" | custom-call | tf_op jit(solution)/shard_map/pallas_call | solution.py:262
